TPU v7x, 512 devices: a whole 4x4x16 slice. The times are simulated.
512 devices in a mesh: pipe: 4 (over z_hi), dp: 16 (over y, x), tensor: 8 (over z_lo, core).
Axes of the slice: x: 4, y: 4, z: 16 (z_hi: 4, z_lo: 4; z = z_hi * 4 + z_lo), core: 2. Of those that a mesh axis runs over, the one named last changes fastest.
Arguments:
- x_in: bfloat16 [4, 2, 16, 128, 1600], P('pipe', None, 'dp', 'tensor'), may hold values from -6 to 6
- out_grad: bfloat16 [2, 16, 128, 1600], P(None, 'dp'), may hold values from -6 to 6
- layer_scale: float32 [4, 1600], P('pipe'), may hold values from 0.05 to 1
- norm_gain: float32 [4, 1600], P('pipe'), may hold values from 0.5 to 1.5
- master: float32 [4, 1600, 8192], P('pipe', 'dp', 'tensor'), may hold values from -0.15625 to 0.15625
- moment_one: float32 [4, 1600, 8192], P('pipe', 'dp', 'tensor'), may hold values from -4 to 4
- moment_two: float32 [4, 1600, 8192], P('pipe', 'dp', 'tensor'), may hold values from 0.05 to 5
Outputs:
- input_grads: bfloat16 [4, 2, 16, 128, 1600], P('pipe', None, 'dp', 'tensor')
- new_master: float32 [4, 1600, 8192], P('pipe', 'dp', 'tensor')
- new_moment_one: float32 [4, 1600, 8192], P('pipe', 'dp', 'tensor')
- new_moment_two: float32 [4, 1600, 8192], P('pipe', 'dp', 'tensor')
- scale_grads: float32 [4, 2, 1600], P('pipe')
All inputs are finite; a program needn't handle non-finite values.
Results may differ from a plain program's by a relative error of at most 0.027.
Values may be sent and summed in bfloat16 or wider, within the bound.
A program may use at most 128 MiB of HBM per device.

v0:
```python
import math
import jax
import jax.numpy as jnp
from jax import lax
from jax.sharding import PartitionSpec as P

HD = 128
beta_one = 0.9
beta_two = 0.95
adam_eps = 1e-08
learn_rate = 0.001
weight_decay = 0.05
adam_step = 100.0
norm_eps = 1e-06


def from_behind(block, axis, distance):
    devices = range(lax.axis_size(axis))
    route = [(i - distance, i) for i in devices if i - distance in devices]
    return lax.ppermute(block, axis, route)


def normalize(values_in):
    inverse = lax.rsqrt(jnp.mean(values_in * values_in, axis=-1, keepdims=True) + norm_eps)
    return (inverse, values_in * inverse)


def select_micro(array, micro_index):
    return lax.dynamic_index_in_dim(array, micro_index, 0, keepdims=False)


def store_slot(buffer, value, slot_index):
    return lax.dynamic_update_index_in_dim(buffer, value, slot_index, 0)


def local(x_in, out_grad, layer_scale, norm_gain, master, moment_one, moment_two):
    n_pipe = lax.axis_size("pipe")
    n_tensor = lax.axis_size("tensor")
    pipe_rank = lax.axis_index("pipe")
    micro_count = x_in.shape[1]
    images = x_in.shape[2]
    shard_len = x_in.shape[3]
    channels = x_in.shape[4]
    seq_len = shard_len * n_tensor
    row_start = lax.axis_index("tensor") * shard_len
    head_cols = master.shape[2] // 4
    local_heads = head_cols // HD
    score_root = math.sqrt(HD)
    scale_vec = layer_scale[0]
    gain_vec = norm_gain[0]
    weights = lax.all_gather(master[0].astype(jnp.bfloat16), "dp", axis=0, tiled=True)
    w_qkv = weights[:, : 3 * head_cols]
    w_out = weights[:, 3 * head_cols :]
    full_x = lax.all_gather(x_in[0], "tensor", axis=2, tiled=True).astype(jnp.float32)
    full_inverse, full_unit = normalize(full_x)
    normed = (full_unit * gain_vec).astype(jnp.bfloat16)
    local_unit = lax.dynamic_slice_in_dim(full_unit, row_start, shard_len, 2)
    local_inverse = lax.dynamic_slice_in_dim(full_inverse, row_start, shard_len, 2)
    projected = jnp.einsum(
        "mbsd,dc->mbsc", normed, w_qkv, preferred_element_type=jnp.float32
    ).astype(jnp.bfloat16)
    projected = projected.reshape(micro_count, images, seq_len, 3, local_heads, HD)
    query = projected[:, :, :, 0]
    keys = projected[:, :, :, 1]
    values = projected[:, :, :, 2]
    scores = (
        jnp.einsum("mbqhe,mbkhe->mbhqk", query, keys, preferred_element_type=jnp.float32)
        / score_root
    )
    probs = jax.nn.softmax(scores, axis=-1)
    probs_low = probs.astype(jnp.bfloat16)
    attended = jnp.einsum(
        "mbhqk,mbkhe->mbqhe", probs_low, values, preferred_element_type=jnp.float32
    ).astype(jnp.bfloat16)
    attended_flat = attended.reshape(micro_count, images, seq_len, head_cols)

    def backward_segment(micro_index, incoming):
        query_now = select_micro(query, micro_index)
        keys_now = select_micro(keys, micro_index)
        values_now = select_micro(values, micro_index)
        probs_now = select_micro(probs, micro_index)
        probs_low_now = select_micro(probs_low, micro_index)
        attended_now = select_micro(attended, micro_index)
        scaled = (scale_vec * incoming.astype(jnp.float32)).astype(jnp.bfloat16)
        d_att = jnp.einsum("bsd,dc->bsc", scaled, w_out, preferred_element_type=jnp.float32).astype(
            jnp.bfloat16
        )
        d_att = d_att.reshape(images, seq_len, local_heads, HD)
        d_prob = jnp.einsum(
            "bqhe,bkhe->bhqk", d_att, values_now, preferred_element_type=jnp.float32
        )
        row_delta = jnp.einsum(
            "bqhe,bqhe->bhq", d_att, attended_now, preferred_element_type=jnp.float32
        )
        d_score = (probs_now * (d_prob - row_delta[..., None]) / score_root).astype(jnp.bfloat16)
        d_query = jnp.einsum(
            "bhqk,bkhe->bqhe", d_score, keys_now, preferred_element_type=jnp.float32
        ).astype(jnp.bfloat16)
        d_keys = jnp.einsum(
            "bhqk,bqhe->bkhe", d_score, query_now, preferred_element_type=jnp.float32
        ).astype(jnp.bfloat16)
        d_values = jnp.einsum(
            "bhqk,bqhe->bkhe", probs_low_now, d_att, preferred_element_type=jnp.float32
        ).astype(jnp.bfloat16)
        d_proj = jnp.concatenate([d_query, d_keys, d_values], axis=2).reshape(
            images, seq_len, 3 * head_cols
        )
        partial_sum = jnp.einsum("bsc,dc->bsd", d_proj, w_qkv, preferred_element_type=jnp.float32)
        return (partial_sum, d_proj, scaled)

    def spare_segment(micro_index, incoming):
        return (
            jnp.zeros((images, seq_len, channels), jnp.float32),
            jnp.zeros((images, seq_len, 3 * head_cols), jnp.bfloat16),
            jnp.zeros((images, seq_len, channels), jnp.bfloat16),
        )

    segments = n_pipe + micro_count - 1
    is_last = pipe_rank == n_pipe - 1
    received = jnp.zeros((images, seq_len, channels), jnp.bfloat16)
    slots = micro_count + 1
    grads_out = jnp.zeros((slots, images, shard_len, channels), jnp.bfloat16)
    proj_saved = jnp.zeros((slots, images, seq_len, 3 * head_cols), jnp.bfloat16)
    scaled_saved = jnp.zeros((slots, images, seq_len, channels), jnp.bfloat16)
    grad_saved = jnp.zeros((slots, images, seq_len, channels), jnp.bfloat16)
    gain_part = jnp.zeros((channels,), jnp.float32)
    for segment_step in range(segments):
        micro_index = segment_step - (n_pipe - 1) + pipe_rank
        active = jnp.logical_and(micro_index >= 0, micro_index < micro_count)
        micro_index = jnp.clip(micro_index, 0, micro_count - 1)
        slot_index = jnp.where(active, micro_index, micro_count)
        arrived = received
        incoming = jnp.where(is_last, select_micro(out_grad, micro_index), arrived)
        partial_sum, d_proj, scaled = lax.cond(
            active, backward_segment, spare_segment, micro_index, incoming
        )
        pieces = partial_sum.astype(jnp.bfloat16).reshape(images, n_tensor, shard_len, channels)
        landed = lax.all_to_all(pieces, "tensor", split_axis=1, concat_axis=1, tiled=True)
        own_d = jnp.sum(landed.astype(jnp.float32), axis=1)
        own_unit = select_micro(local_unit, micro_index)
        own_inverse = select_micro(local_inverse, micro_index)
        d_unit = own_d * gain_vec
        d_input = own_inverse * (
            d_unit - own_unit * jnp.mean(d_unit * own_unit, axis=-1, keepdims=True)
        )
        own_incoming = lax.dynamic_slice_in_dim(incoming, row_start, shard_len, 1)
        own_passed = (own_incoming.astype(jnp.float32) + d_input).astype(jnp.bfloat16)
        gain_part = gain_part + jnp.where(active, jnp.sum(own_d * own_unit, axis=(0, 1)), 0.0)
        grads_out = store_slot(grads_out, own_passed, slot_index)
        proj_saved = store_slot(proj_saved, d_proj, slot_index)
        scaled_saved = store_slot(scaled_saved, scaled, slot_index)
        grad_saved = store_slot(grad_saved, incoming, slot_index)
        if segment_step + 1 < segments:
            moved = from_behind(own_passed, "pipe", -1)
            received = lax.all_gather(moved, "tensor", axis=1, tiled=True)
    grads_kept = grads_out[:micro_count]
    proj_kept = proj_saved[:micro_count]
    scaled_kept = scaled_saved[:micro_count]
    grad_kept = grad_saved[:micro_count]
    grad_qkv = jnp.einsum("mbsd,mbsc->dc", normed, proj_kept, preferred_element_type=jnp.float32)
    grad_out = jnp.einsum(
        "mbsd,mbsc->dc", scaled_kept, attended_flat, preferred_element_type=jnp.float32
    )
    weight_grad = lax.psum_scatter(
        jnp.concatenate([grad_qkv, grad_out], axis=1).astype(jnp.bfloat16),
        "dp",
        scatter_dimension=0,
        tiled=True,
    ).astype(jnp.float32)
    summed_out = jnp.einsum(
        "mbsd,mbsc->dc", grad_kept, attended_flat, preferred_element_type=jnp.float32
    )
    scale_part = jnp.sum(w_out.astype(jnp.float32) * summed_out, axis=1)
    scale_both = lax.psum(lax.psum(jnp.stack([scale_part, gain_part]), "tensor"), "dp")
    bias_one = 1.0 - beta_one**adam_step
    bias_two = 1.0 - beta_two**adam_step
    first_new = beta_one * moment_one[0] + (1.0 - beta_one) * weight_grad
    second_new = beta_two * moment_two[0] + (1.0 - beta_two) * weight_grad * weight_grad
    update = first_new / bias_one / (jnp.sqrt(second_new / bias_two) + adam_eps)
    master_new = master[0] - learn_rate * (update + weight_decay * master[0])
    return (grads_kept[None], master_new[None], first_new[None], second_new[None], scale_both[None])


def solution(mesh):
    placed = (
        P("pipe", None, "dp", "tensor", None),
        P(None, "dp", None, None),
        P("pipe", None),
        P("pipe", None),
        P("pipe", "dp", "tensor"),
        P("pipe", "dp", "tensor"),
        P("pipe", "dp", "tensor"),
    )
    return jax.shard_map(
        local,
        mesh=mesh,
        in_specs=placed,
        out_specs=(
            P("pipe", None, "dp", "tensor", None),
            P("pipe", "dp", "tensor"),
            P("pipe", "dp", "tensor"),
            P("pipe", "dp", "tensor"),
            P("pipe", None, None),
        ),
        check_vma=False,
    )
```

profile of v0, /device:TPU:128, one launch (start us, length us, event | category | flops | bytes accessed | tf_op | source)
XLA Modules:
  0.0 831.2 jit_solution(14182584001447104835)
XLA Ops:
  9.8 17.2 %all-gather = bf16[1,2,1,128,1600]{4,3,2,1,0:T(8,128)(2,1)S(1)} all-gather(bf16[1,2,1,16,1600]{4,3,2,1,0:T(8,128)(2,1)} %param.17), channel_id=2, replica_groups=mesh['pipe'=4,'dp'=16,'tensor'=8] {'tensor'}, dimensions={3}, use_global_device_ids=true | all-gather | bytes 921600 | tf_op jit(solution)/shard_map/all_gather | solution.py:54
  28.4 50.3 %all-gather.4.cloned.1.call-done = bf16[16,100,1024]{2,1,0:T(8,128)(2,1)} async-done(((bf16[1,100,1024]{2,1,0:T(8,128)(2,1)}), bf16[16,100,1024]{2,1,0:T(8,128)(2,1)}) %all-gather.4.cloned.1.call-update) | async-done | bytes 3276816 | tf_op jit(solution)/shard_map/all_gather | solution.py:51
  78.8 4.5 reshape.1362
  84.5 2.6 fusion.115
  95.5 2.3 conditional.5
  99.8 4.8 all-to-all-start
  106.1 2.5 convert_multiply_fusion.6
  108.6 9.3 %all-to-all-done = bf16[1,8,16,1600]{3,2,0,1:T(8,128)(2,1)} async-done(((bf16[1,8,16,1600]{3,2,0,1:T(8,128)(2,1)}), bf16[1,8,16,1600]{3,2,0,1:T(8,128)(2,1)}, u32[]{:S(2)}, u32[]{:S(2)}) %all-to-all-start) | async-done | bytes 409632 | tf_op jit(solution)/shard_map/all_to_all | solution.py:138
  121.8 2.2 fusion.165
  128.0 2.2 fusion.121
  130.1 2.1 collective-permute-start
  132.2 40.1 %collective-permute-done = bf16[1,16,1600]{1,2,0:T(8,128)(2,1)} collective-permute-done((bf16[1,16,1600]{1,2,0:T(8,128)(2,1)}, bf16[1,16,1600]{1,2,0:T(8,128)(2,1)}, u32[]{:S(2)}, u32[]{:S(2)}) %collective-permute-start) | collective-permute-done | bytes 51232 | tf_op jit(solution)/shard_map/ppermute | solution.py:20
  174.1 15.8 %all_gather.20 = bf16[1,128,1600]{2,1,0:T(8,128)(2,1)} all-gather(bf16[1,16,1600]{2,1,0:T(8,128)(2,1)} %copy.219), channel_id=1, replica_groups=mesh['pipe'=4,'dp'=16,'tensor'=8] {'tensor'}, dimensions={1}, use_global_device_ids=true | all-gather | bytes 460800 | tf_op jit(solution)/shard_map/all_gather | solution.py:155
  191.9 2.1 bitcast_dynamic-update-slice_fusion.2
  194.0 2.7 conditional.6
  198.7 16.6 %all_to_all.25 = bf16[1,8,16,1600]{3,2,0,1:T(8,128)(2,1)S(1)} all-to-all(bf16[1,8,16,1600]{3,2,0,1:T(8,128)(2,1)} %bitcast.592), channel_id=1, replica_groups=mesh['pipe'=4,'dp'=16,'tensor'=8] {'tensor'}, dimensions={1} | all-to-all | bytes 819200 | tf_op jit(solution)/shard_map/all_to_all | solution.py:138
  216.1 2.2 fusion.164
  224.3 2.2 fusion.141
  226.4 2.2 collective-permute-start.1
  228.6 94.0 %collective-permute-done.1 = bf16[1,16,1600]{1,2,0:T(8,128)(2,1)} collective-permute-done((bf16[1,16,1600]{1,2,0:T(8,128)(2,1)}, bf16[1,16,1600]{1,2,0:T(8,128)(2,1)}, u32[]{:S(2)}, u32[]{:S(2)}) %collective-permute-start.1) | collective-permute-done | bytes 51232 | tf_op jit(solution)/shard_map/ppermute | solution.py:20
  324.4 15.8 %all_gather.21 = bf16[1,128,1600]{2,1,0:T(8,128)(2,1)} all-gather(bf16[1,16,1600]{2,1,0:T(8,128)(2,1)} %copy.234), channel_id=1, replica_groups=mesh['pipe'=4,'dp'=16,'tensor'=8] {'tensor'}, dimensions={1}, use_global_device_ids=true | all-gather | bytes 460800 | tf_op jit(solution)/shard_map/all_gather | solution.py:155
  342.2 2.1 bitcast_dynamic-update-slice_fusion.1
  344.3 32.0 %conditional.7 = (bf16[1,128,1600]{1,2,0:T(8,128)(2,1)}, bf16[1,1,128,768]{3,2,0,1:T(8,128)(2,1)}, bf16[1,1,128,1600]{2,3,0,1:T(8,128)(2,1)}) conditional(s32[]{:T(128)} %convert_element_type.339, () %tuple.72, (s32[]{:T(128)}, bf16[2,1,128,2,128]{4,2,3,0,1:T(8,128)(2,1)}, f32[2,1,2,128,128]{3,4,2,0,1:T(8,128)S(1)}, f32[1,1600]{1,0:T(1,128)S(1)}, ...), branch_computations={%region_11.12_spmd, %region_12.13_spmd} | conditional | flops 454803200 | bytes 11565162 | solution.py:134
  378.3 4.1 all-to-all-start.2
  391.7 4.0 all-to-all-done.2
  397.4 2.2 fusion.163
  399.6 2.1 copy.246
  401.7 2.2 copy.247
  411.1 38.8 %collective-permute-done.2 = bf16[1,16,1600]{1,2,0:T(8,128)(2,1)} collective-permute-done((bf16[1,16,1600]{1,2,0:T(8,128)(2,1)S(1)}, bf16[1,16,1600]{1,2,0:T(8,128)(2,1)}, u32[]{:S(2)}, u32[]{:S(2)}) %collective-permute-start.2) | collective-permute-done | bytes 51232 | tf_op jit(solution)/shard_map/ppermute | solution.py:20
  451.8 15.8 %all_gather.22 = bf16[1,128,1600]{2,1,0:T(8,128)(2,1)} all-gather(bf16[1,16,1600]{2,1,0:T(8,128)(2,1)} %copy.249), channel_id=1, replica_groups=mesh['pipe'=4,'dp'=16,'tensor'=8] {'tensor'}, dimensions={1}, use_global_device_ids=true | all-gather | bytes 460800 | tf_op jit(solution)/shard_map/all_gather | solution.py:155
  469.5 2.1 bitcast_dynamic-update-slice_fusion
  471.6 32.2 %conditional.8 = (bf16[1,128,1600]{1,2,0:T(8,128)(2,1)}, bf16[1,1,128,768]{3,2,0,1:T(8,128)(2,1)}, bf16[1,1,128,1600]{2,3,0,1:T(8,128)(2,1)}) conditional(s32[]{:T(128)} %convert_element_type.344, () %tuple.74, (s32[]{:T(128)}, bf16[2,1,128,2,128]{4,2,3,0,1:T(8,128)(2,1)}, f32[2,1,2,128,128]{3,4,2,0,1:T(8,128)S(1)}, f32[1,1600]{1,0:T(1,128)S(1)}, ...), branch_computations={%region_15.16_spmd, %region_16.17_spmd} | conditional | flops 454803200 | bytes 11565162 | solution.py:134
  505.9 4.1 all-to-all-start.3
  528.4 2.2 fusion.162
  530.6 2.1 copy.261
  532.7 2.2 copy.262
  536.7 2.2 fusion.131
  538.9 2.2 collective-permute-start.3
  544.3 14.5 %collective-permute-done.3 = bf16[1,16,1600]{1,2,0:T(8,128)(2,1)} collective-permute-done((bf16[1,16,1600]{1,2,0:T(8,128)(2,1)}, bf16[1,16,1600]{1,2,0:T(8,128)(2,1)}, u32[]{:S(2)}, u32[]{:S(2)}) %collective-permute-start.3) | collective-permute-done | bytes 51232 | tf_op jit(solution)/shard_map/ppermute | solution.py:20
  560.6 37.5 %all_gather.23 = bf16[1,128,1600]{2,1,0:T(8,128)(2,1)} all-gather(bf16[1,16,1600]{2,1,0:T(8,128)(2,1)} %copy.264), channel_id=1, replica_groups=mesh['pipe'=4,'dp'=16,'tensor'=8] {'tensor'}, dimensions={1}, use_global_device_ids=true | all-gather | bytes 460800 | tf_op jit(solution)/shard_map/all_gather | solution.py:155
  600.0 2.1 bitcast_dynamic-update-slice_fusion.3
  602.1 2.3 conditional.9
  606.5 5.1 all-to-all-start.4
  619.0 85.0 %fusion = bf16[112,1024]{1,0:T(8,128)(2,1)} fusion(bf16[1600,1024]{1,0:T(8,128)(2,1)S(1)} %pad_maximum_fusion.5), kind=kCustom, calls=%all-reduce-scatter | all-reduce-scatter fusion | flops 1835009 | bytes 3508224
  705.0 3.7 collective-permute-start.4
  708.6 4.1 collective-permute-start.5
  722.6 27.0 %psum.14 = f32[2,1600]{1,0:T(2,128)S(1)} all-reduce(f32[2,1600]{1,0:T(2,128)S(1)} %pad_maximum_fusion.6), channel_id=1, replica_groups=mesh['pipe'=4,'dp'=16,'tensor'=8] {'tensor'}, use_global_device_ids=true, to_apply=%region_30.31 | all-reduce | flops 3200 | bytes 25600 | tf_op jit(solution)/shard_map/psum | solution.py:174
  749.6 71.2 %psum.15 = f32[1,2,1600]{2,1,0:T(2,128)} all-reduce(f32[1,2,1600]{2,1,0:T(2,128)S(1)} %bitcast.594), channel_id=1, replica_groups=mesh['pipe'=4,'dp'=16,'tensor'=8] {'dp'}, use_global_device_ids=true, to_apply=%region_31.32 | all-reduce | flops 3200 | bytes 25600 | tf_op jit(solution)/shard_map/psum | solution.py:174
  (224 shorter events, 187.9 us)
Async XLA Ops:
  7.2 71.6 %all-gather.4.cloned.1.call-start = ((), (), s32[]{:S(2)}) async-start(), calls=%async_computation.5 | async-start | bytes 3620864 | tf_op jit(solution)/shard_map/all_gather | solution.py:51
  9.0 18.5 %copy-start.10 = (bf16[2,1,128,1600]{2,3,1,0:T(8,128)(2,1)S(1)}, bf16[2,1,128,1600]{2,3,1,0:T(8,128)(2,1)}, u32[]{:S(2)}) copy-start(bf16[2,1,128,1600]{2,3,1,0:T(8,128)(2,1)} %param.18) | copy-start | bytes 2457604
  27.0 57.4 %copy-start = (bf16[1,2,1,128,1600]{4,3,2,1,0:T(8,128)(2,1)}, bf16[1,2,1,128,1600]{4,3,2,1,0:T(8,128)(2,1)S(1)}, u32[]{:S(2)}) copy-start(bf16[1,2,1,128,1600]{4,3,2,1,0:T(8,128)(2,1)S(1)} %all-gather) | copy-start | bytes 2457604
  27.3 57.2 %copy-start.39 = (f32[2,128]{1,0:T(2,128)}, f32[2,128]{1,0:T(2,128)S(1)}, u32[]{:S(2)}) copy-start(f32[2,128]{1,0:T(2,128)S(1)} %add_rsqrt_fusion) | copy-start | bytes 3076
  28.4 50.4 %copy-start.21 = (bf16[3,1,128,1600]{2,3,0,1:T(8,128)(2,1)}, bf16[3,1,128,1600]{2,3,0,1:T(8,128)(2,1)S(1)}, u32[]{:S(2)}) copy-start(bf16[3,1,128,1600]{2,3,0,1:T(8,128)(2,1)S(1)} %get-tuple-element.409) | copy-start | bytes 3686404
  87.5 0.8 copy-start.27
  87.5 4.2 copy-start.26
  91.7 3.9 copy-start.33
  91.8 2.1 copy-start.12
  99.8 18.2 %all-to-all-start = ((bf16[1,8,16,1600]{3,2,0,1:T(8,128)(2,1)}), bf16[1,8,16,1600]{3,2,0,1:T(8,128)(2,1)}, u32[]{:S(2)}, u32[]{:S(2)}) async-start(bf16[1,8,16,1600]{3,2,0,1:T(8,128)(2,1)} %bitcast.589), calls=%async_computation | async-start | bytes 851968 | tf_op jit(solution)/shard_map/all_to_all | solution.py:138
  126.1 1.8 copy-start.2
  126.1 1.9 copy-start.6
  130.1 42.2 %collective-permute-start = (bf16[1,16,1600]{1,2,0:T(8,128)(2,1)}, bf16[1,16,1600]{1,2,0:T(8,128)(2,1)}, u32[]{:S(2)}, u32[]{:S(2)}) collective-permute-start(bf16[1,16,1600]{1,2,0:T(8,128)(2,1)} %fusion.121), channel_id=1, source_target_pairs={{128,0},{256,128},{384,256},{129,1},{257,129},{385,257},{130,2},{2... | collective-permute-start | bytes 153608 | tf_op jit(solution)/shard_map/ppermute | solution.py:20
  215.4 0.7 copy-start.22
  222.4 1.8 copy-start.3
  222.4 1.9 copy-start.7
  226.4 96.2 %collective-permute-start.1 = (bf16[1,16,1600]{1,2,0:T(8,128)(2,1)}, bf16[1,16,1600]{1,2,0:T(8,128)(2,1)}, u32[]{:S(2)}, u32[]{:S(2)}) collective-permute-start(bf16[1,16,1600]{1,2,0:T(8,128)(2,1)} %fusion.141), channel_id=1, source_target_pairs={{128,0},{256,128},{384,256},{129,1},{257,129},{385,257},{130,2},{2... | collective-permute-start | bytes 153608 | tf_op jit(solution)/shard_map/ppermute | solution.py:20
  372.3 0.7 copy-start.16
  378.3 17.4 %all-to-all-start.2 = ((bf16[1,8,16,1600]{3,2,0,1:T(8,128)(2,1)}), bf16[1,8,16,1600]{3,2,0,1:T(8,128)(2,1)}, u32[]{:S(2)}, u32[]{:S(2)}) async-start(bf16[1,8,16,1600]{3,2,0,1:T(8,128)(2,1)} %bitcast.590), calls=%async_computation.2 | async-start | bytes 851968 | tf_op jit(solution)/shard_map/all_to_all | solution.py:138
  396.8 0.6 copy-start.23
  403.9 1.8 copy-start.4
  403.9 1.9 copy-start.8
  405.7 4.8 copy-start.32
  407.2 0.8 copy-start.18
  407.9 42.0 %collective-permute-start.2 = (bf16[1,16,1600]{1,2,0:T(8,128)(2,1)S(1)}, bf16[1,16,1600]{1,2,0:T(8,128)(2,1)}, u32[]{:S(2)}, u32[]{:S(2)}) collective-permute-start(bf16[1,16,1600]{1,2,0:T(8,128)(2,1)S(1)} %fusion.136), channel_id=1, source_target_pairs={{128,0},{256,128},{384,256},{129,1},{257,129},{385,257},{130,2},{2... | collective-permute-start | bytes 153608 | tf_op jit(solution)/shard_map/ppermute | solution.py:20
  499.9 0.7 copy-start.17
  505.9 20.8 %all-to-all-start.3 = ((bf16[1,8,16,1600]{3,2,0,1:T(8,128)(2,1)}), bf16[1,8,16,1600]{3,2,0,1:T(8,128)(2,1)}, u32[]{:S(2)}, u32[]{:S(2)}) async-start(bf16[1,8,16,1600]{3,2,0,1:T(8,128)(2,1)} %bitcast.591), calls=%async_computation.3 | async-start | bytes 851968 | tf_op jit(solution)/shard_map/all_to_all | solution.py:138
  527.8 0.6 copy-start.24
  534.8 1.8 copy-start.5
  534.8 1.9 copy-start.9
  538.9 19.9 %collective-permute-start.3 = (bf16[1,16,1600]{1,2,0:T(8,128)(2,1)}, bf16[1,16,1600]{1,2,0:T(8,128)(2,1)}, u32[]{:S(2)}, u32[]{:S(2)}) collective-permute-start(bf16[1,16,1600]{1,2,0:T(8,128)(2,1)} %fusion.131), channel_id=1, source_target_pairs={{128,0},{256,128},{384,256},{129,1},{257,129},{385,257},{130,2},{2... | collective-permute-start | bytes 153608 | tf_op jit(solution)/shard_map/ppermute | solution.py:20
  604.4 8.8 %copy-start.1 = (bf16[1,2,1,128,1600]{4,3,2,1,0:T(8,128)(2,1)S(1)}, bf16[1,2,1,128,1600]{4,3,2,1,0:T(8,128)(2,1)}, u32[]{:S(2)}) copy-start(bf16[1,2,1,128,1600]{4,3,2,1,0:T(8,128)(2,1)} %copy-done) | copy-start | bytes 2457604
  604.4 8.8 %copy-start.40 = (f32[2,128]{1,0:T(2,128)S(1)}, f32[2,128]{1,0:T(2,128)}, u32[]{:S(2)}) copy-start(f32[2,128]{1,0:T(2,128)} %copy-done.39) | copy-start | bytes 3076
  606.5 113.7 %all-to-all-start.4 = ((bf16[1,8,16,1600]{3,2,0,1:T(8,128)(2,1)}), bf16[1,8,16,1600]{3,2,0,1:T(8,128)(2,1)}, u32[]{:S(2)}, u32[]{:S(2)}) async-start(bf16[1,8,16,1600]{3,2,0,1:T(8,128)(2,1)} %bitcast.152), calls=%async_computation.4 | async-start | bytes 851968 | tf_op jit(solution)/shard_map/all_to_all | solution.py:138
  613.2 3.7 copy-start.11
  704.0 11.5 %copy-start.20 = (bf16[112,1024]{1,0:T(8,128)(2,1)S(1)}, bf16[112,1024]{1,0:T(8,128)(2,1)}, u32[]{:S(2)}) copy-start(bf16[112,1024]{1,0:T(8,128)(2,1)} %fusion) | copy-start | bytes 688132
  705.0 10.5 %collective-permute-start.4 = (bf16[112,1024]{1,0:T(8,128)(2,1)}, bf16[112,1024]{1,0:T(8,128)(2,1)S(1)}, u32[]{:S(2)}, u32[]{:S(2)}) collective-permute-start(bf16[112,1024]{1,0:T(8,128)(2,1)} %fusion), channel_id=1, source_target_pairs={{0,8},{8,16},{16,24},{24,32},{32,40},{40,48},{48,56},{56,64},{64,7... | collective-permute-start | bytes 688136
  708.6 6.8 collective-permute-start.5
  712.7 3.4 copy-start.19
  712.7 3.4 copy-start.28
  712.7 3.4 copy-start.29
  717.8 4.7 copy-start.35
  717.8 4.7 copy-start.36
  717.8 4.7 copy-start.37
  717.8 4.7 copy-start.38
  722.2 99.2 %copy-start.13 = (bf16[1,128,1600]{1,2,0:T(8,128)(2,1)S(1)}, bf16[1,128,1600]{1,2,0:T(8,128)(2,1)}, u32[]{:S(2)}) copy-start(bf16[1,128,1600]{1,2,0:T(8,128)(2,1)} %get-tuple-element.402) | copy-start | bytes 1228804
  722.2 99.2 %copy-start.41 = (f32[16]{0:T(128)S(1)}, f32[16]{0:T(128)}, u32[]{:S(2)}) copy-start(f32[16]{0:T(128)} %get-tuple-element.429) | copy-start | bytes 196
Sparse Core Ops, SparseCore 0:
  11.6 67.1 all-gather.3
where the time goes:
time: 842 us; the launch traced here: 831 us
  blocking collectives  302 us (36%)
  waiting for transfers between devices  252 us (30%)
  local copies, waits for them, and re-layouts  145 us (17%)
  other arithmetic  54.5 us (6%)
  starting transfers between devices  34.3 us (4%)
  matrix products  27.2 us (3%)
  between operations  15.5 us (2%)
    ppermute x4, waiting for transfers between devices, from_behind(): return lax.ppermute(block, axis, route)  187 us
    unnamed x1, blocking collectives  85 us
    all_gather x4, blocking collectives, local(): received = lax.all_gather(moved, 'tensor', axis=1, tiled=True)  84.8 us
    psum x1, blocking collectives, local(): lax.psum(lax.psum(jnp.stack([scale_part, gain_part]), 'tensor'), 'dp')  71.2 us
    all_gather x1, waiting for transfers between devices, local(): lax.all_gather(master[0].astype(jnp.bfloat16), 'dp', axis=0, tiled=True)  50.3 us
    another operation x23, local copies, waits for them, and re-layouts  32.2 us
    psum x1, blocking collectives, local(): lax.psum(jnp.stack([scale_part, gain_part]), 'tensor')  27 us
    dynamic_update_slice x15, local copies, waits for them, and re-layouts, store_slot(): return lax.dynamic_update_index_in_dim(buffer, value, slot_index, 0)  22.6 us
  transfers between devices with their start and end apart: 11, of which 8 were waited for; matrix products, arithmetic and copies ran while one was open for 16% of the time, Pallas kernels for 0%

commit v1 on v0

--- a/solution.py
+++ b/solution.py
@@ -171,7 +171,9 @@
         "mbsd,mbsc->dc", grad_kept, attended_flat, preferred_element_type=jnp.float32
     )
     scale_part = jnp.sum(w_out.astype(jnp.float32) * summed_out, axis=1)
-    scale_both = lax.psum(lax.psum(jnp.stack([scale_part, gain_part]), "tensor"), "dp")
+    part = lax.psum(jnp.stack([scale_part, gain_part]), "tensor")
+    terms = lax.all_gather(part, "dp", axis=0, tiled=False)
+    scale_both = terms.sum(axis=0)
     bias_one = 1.0 - beta_one**adam_step
     bias_two = 1.0 - beta_two**adam_step
     first_new = beta_one * moment_one[0] + (1.0 - beta_one) * weight_grad

time: 842 us -> 796 us (0.945)
  blocking collectives: 302 us -> 255 us
    psum x2 -> x1, blocking collectives: 98.2 us -> 27 us  [local(): part = lax.psum(jnp.stack([scale_part, gain_part]), 'tensor')]
    all_gather x0 -> x1, blocking collectives: none -> 24.6 us  [local(): terms = lax.all_gather(part, 'dp', axis=0, tiled=False)]
  transfers between devices with their start and end apart: 11 -> 11, of which waited for: 8 -> 8; matrix products, arithmetic and copies ran while one was open for 16% -> 17% of each run, Pallas kernels for 0% -> 0%
where the time goes in v1:
time: 796 us; the launch traced here: 785 us
  blocking collectives  255 us (32%)
  waiting for transfers between devices  252 us (32%)
  local copies, waits for them, and re-layouts  145 us (18%)
  other arithmetic  55.2 us (7%)
  starting transfers between devices  34.3 us (4%)
  matrix products  27.2 us (3%)
  between operations  15.5 us (2%)
    ppermute x4, waiting for transfers between devices, from_behind(): return lax.ppermute(block, axis, route)  187 us
    unnamed x1, blocking collectives  85 us
    all_gather x4, blocking collectives, local(): received = lax.all_gather(moved, 'tensor', axis=1, tiled=True)  84.8 us
    all_gather x1, waiting for transfers between devices, local(): lax.all_gather(master[0].astype(jnp.bfloat16), 'dp', axis=0, tiled=True)  50.3 us
    another operation x23, local copies, waits for them, and re-layouts  32.2 us
    psum x1, blocking collectives, local(): part = lax.psum(jnp.stack([scale_part, gain_part]), 'tensor')  27 us
    all_gather x1, blocking collectives, local(): terms = lax.all_gather(part, 'dp', axis=0, tiled=False)  24.6 us
    dynamic_update_slice x15, local copies, waits for them, and re-layouts, store_slot(): return lax.dynamic_update_index_in_dim(buffer, value, slot_index, 0)  22.6 us
  transfers between devices with their start and end apart: 11, of which 8 were waited for; matrix products, arithmetic and copies ran while one was open for 17% of the time, Pallas kernels for 0%

profile of v1, /device:TPU:128, one launch (start us, length us, event | category | flops | bytes accessed | tf_op | source)
XLA Modules:
  0.0 785.3 jit_solution(4144338740636004742)
XLA Ops:
  9.8 17.2 %all-gather = bf16[1,2,1,128,1600]{4,3,2,1,0:T(8,128)(2,1)S(1)} all-gather(bf16[1,2,1,16,1600]{4,3,2,1,0:T(8,128)(2,1)} %param.17), channel_id=2, replica_groups=mesh['pipe'=4,'dp'=16,'tensor'=8] {'tensor'}, dimensions={3}, use_global_device_ids=true | all-gather | bytes 921600 | tf_op jit(solution)/shard_map/all_gather | solution.py:54
  28.4 50.3 %all-gather.4.cloned.1.call-done = bf16[16,100,1024]{2,1,0:T(8,128)(2,1)} async-done(((bf16[1,100,1024]{2,1,0:T(8,128)(2,1)}), bf16[16,100,1024]{2,1,0:T(8,128)(2,1)}) %all-gather.4.cloned.1.call-update) | async-done | bytes 3276816 | tf_op jit(solution)/shard_map/all_gather | solution.py:51
  78.8 4.5 reshape.1362
  84.5 2.6 fusion.115
  95.5 2.3 conditional.5
  99.8 4.8 all-to-all-start
  106.1 2.5 convert_multiply_fusion.6
  108.6 9.3 %all-to-all-done = bf16[1,8,16,1600]{3,2,0,1:T(8,128)(2,1)} async-done(((bf16[1,8,16,1600]{3,2,0,1:T(8,128)(2,1)}), bf16[1,8,16,1600]{3,2,0,1:T(8,128)(2,1)}, u32[]{:S(2)}, u32[]{:S(2)}) %all-to-all-start) | async-done | bytes 409632 | tf_op jit(solution)/shard_map/all_to_all | solution.py:138
  121.8 2.2 fusion.165
  128.0 2.2 fusion.121
  130.1 2.1 collective-permute-start
  132.2 40.1 %collective-permute-done = bf16[1,16,1600]{1,2,0:T(8,128)(2,1)} collective-permute-done((bf16[1,16,1600]{1,2,0:T(8,128)(2,1)}, bf16[1,16,1600]{1,2,0:T(8,128)(2,1)}, u32[]{:S(2)}, u32[]{:S(2)}) %collective-permute-start) | collective-permute-done | bytes 51232 | tf_op jit(solution)/shard_map/ppermute | solution.py:20
  174.1 15.8 %all_gather.26 = bf16[1,128,1600]{2,1,0:T(8,128)(2,1)} all-gather(bf16[1,16,1600]{2,1,0:T(8,128)(2,1)} %copy.219), channel_id=1, replica_groups=mesh['pipe'=4,'dp'=16,'tensor'=8] {'tensor'}, dimensions={1}, use_global_device_ids=true | all-gather | bytes 460800 | tf_op jit(solution)/shard_map/all_gather | solution.py:155
  191.9 2.1 bitcast_dynamic-update-slice_fusion.2
  194.0 2.7 conditional.6
  198.7 16.6 %all_to_all.25 = bf16[1,8,16,1600]{3,2,0,1:T(8,128)(2,1)S(1)} all-to-all(bf16[1,8,16,1600]{3,2,0,1:T(8,128)(2,1)} %bitcast.594), channel_id=1, replica_groups=mesh['pipe'=4,'dp'=16,'tensor'=8] {'tensor'}, dimensions={1} | all-to-all | bytes 819200 | tf_op jit(solution)/shard_map/all_to_all | solution.py:138
  216.1 2.2 fusion.164
  224.3 2.2 fusion.141
  226.4 2.2 collective-permute-start.1
  228.6 94.0 %collective-permute-done.1 = bf16[1,16,1600]{1,2,0:T(8,128)(2,1)} collective-permute-done((bf16[1,16,1600]{1,2,0:T(8,128)(2,1)}, bf16[1,16,1600]{1,2,0:T(8,128)(2,1)}, u32[]{:S(2)}, u32[]{:S(2)}) %collective-permute-start.1) | collective-permute-done | bytes 51232 | tf_op jit(solution)/shard_map/ppermute | solution.py:20
  324.4 15.8 %all_gather.27 = bf16[1,128,1600]{2,1,0:T(8,128)(2,1)} all-gather(bf16[1,16,1600]{2,1,0:T(8,128)(2,1)} %copy.234), channel_id=1, replica_groups=mesh['pipe'=4,'dp'=16,'tensor'=8] {'tensor'}, dimensions={1}, use_global_device_ids=true | all-gather | bytes 460800 | tf_op jit(solution)/shard_map/all_gather | solution.py:155
  342.2 2.1 bitcast_dynamic-update-slice_fusion.1
  344.3 32.0 %conditional.7 = (bf16[1,128,1600]{1,2,0:T(8,128)(2,1)}, bf16[1,1,128,768]{3,2,0,1:T(8,128)(2,1)}, bf16[1,1,128,1600]{2,3,0,1:T(8,128)(2,1)}) conditional(s32[]{:T(128)} %convert_element_type.339, () %tuple.72, (s32[]{:T(128)}, bf16[2,1,128,2,128]{4,2,3,0,1:T(8,128)(2,1)}, f32[2,1,2,128,128]{3,4,2,0,1:T(8,128)S(1)}, f32[1,1600]{1,0:T(1,128)S(1)}, ...), branch_computations={%region_11.12_spmd, %region_12.13_spmd} | conditional | flops 454803200 | bytes 11565162 | solution.py:134
  378.3 4.1 all-to-all-start.2
  391.7 4.0 all-to-all-done.2
  397.4 2.2 fusion.163
  399.6 2.1 copy.246
  401.7 2.2 copy.247
  411.1 38.8 %collective-permute-done.2 = bf16[1,16,1600]{1,2,0:T(8,128)(2,1)} collective-permute-done((bf16[1,16,1600]{1,2,0:T(8,128)(2,1)S(1)}, bf16[1,16,1600]{1,2,0:T(8,128)(2,1)}, u32[]{:S(2)}, u32[]{:S(2)}) %collective-permute-start.2) | collective-permute-done | bytes 51232 | tf_op jit(solution)/shard_map/ppermute | solution.py:20
  451.8 15.8 %all_gather.28 = bf16[1,128,1600]{2,1,0:T(8,128)(2,1)} all-gather(bf16[1,16,1600]{2,1,0:T(8,128)(2,1)} %copy.249), channel_id=1, replica_groups=mesh['pipe'=4,'dp'=16,'tensor'=8] {'tensor'}, dimensions={1}, use_global_device_ids=true | all-gather | bytes 460800 | tf_op jit(solution)/shard_map/all_gather | solution.py:155
  469.5 2.1 bitcast_dynamic-update-slice_fusion
  471.6 32.2 %conditional.8 = (bf16[1,128,1600]{1,2,0:T(8,128)(2,1)}, bf16[1,1,128,768]{3,2,0,1:T(8,128)(2,1)}, bf16[1,1,128,1600]{2,3,0,1:T(8,128)(2,1)}) conditional(s32[]{:T(128)} %convert_element_type.344, () %tuple.74, (s32[]{:T(128)}, bf16[2,1,128,2,128]{4,2,3,0,1:T(8,128)(2,1)}, f32[2,1,2,128,128]{3,4,2,0,1:T(8,128)S(1)}, f32[1,1600]{1,0:T(1,128)S(1)}, ...), branch_computations={%region_15.16_spmd, %region_16.17_spmd} | conditional | flops 454803200 | bytes 11565162 | solution.py:134
  505.9 4.1 all-to-all-start.3
  528.4 2.2 fusion.162
  530.6 2.1 copy.261
  532.7 2.2 copy.262
  536.7 2.2 fusion.131
  538.9 2.2 collective-permute-start.3
  544.3 14.5 %collective-permute-done.3 = bf16[1,16,1600]{1,2,0:T(8,128)(2,1)} collective-permute-done((bf16[1,16,1600]{1,2,0:T(8,128)(2,1)}, bf16[1,16,1600]{1,2,0:T(8,128)(2,1)}, u32[]{:S(2)}, u32[]{:S(2)}) %collective-permute-start.3) | collective-permute-done | bytes 51232 | tf_op jit(solution)/shard_map/ppermute | solution.py:20
  560.6 37.5 %all_gather.29 = bf16[1,128,1600]{2,1,0:T(8,128)(2,1)} all-gather(bf16[1,16,1600]{2,1,0:T(8,128)(2,1)} %copy.264), channel_id=1, replica_groups=mesh['pipe'=4,'dp'=16,'tensor'=8] {'tensor'}, dimensions={1}, use_global_device_ids=true | all-gather | bytes 460800 | tf_op jit(solution)/shard_map/all_gather | solution.py:155
  600.0 2.1 bitcast_dynamic-update-slice_fusion.3
  602.1 2.3 conditional.9
  606.5 5.1 all-to-all-start.4
  619.0 85.0 %fusion = bf16[112,1024]{1,0:T(8,128)(2,1)} fusion(bf16[1600,1024]{1,0:T(8,128)(2,1)S(1)} %pad_maximum_fusion.5), kind=kCustom, calls=%all-reduce-scatter | all-reduce-scatter fusion | flops 1835009 | bytes 3508224
  705.0 3.7 collective-permute-start.4
  708.6 4.1 collective-permute-start.5
  722.6 27.0 %psum.7 = f32[1,2,1600]{2,1,0:T(2,128)S(1)} all-reduce(f32[1,2,1600]{2,1,0:T(2,128)S(1)} %maximum_bitcast_fusion), channel_id=1, replica_groups=mesh['pipe'=4,'dp'=16,'tensor'=8] {'tensor'}, use_global_device_ids=true, to_apply=%region_30.31 | all-reduce | flops 3200 | bytes 25600 | tf_op jit(solution)/shard_map/psum | solution.py:174
  749.6 24.6 %all_gather.31 = f32[16,2,1600]{2,1,0:T(2,128)S(1)} all-gather(f32[1,2,1600]{2,1,0:T(2,128)S(1)} %psum.7), channel_id=1, replica_groups=mesh['pipe'=4,'dp'=16,'tensor'=8] {'dp'}, dimensions={0}, use_global_device_ids=true | all-gather | bytes 217600 | tf_op jit(solution)/shard_map/all_gather | solution.py:175
  (225 shorter events, 188.5 us)
Async XLA Ops:
  7.2 71.6 %all-gather.4.cloned.1.call-start = ((), (), s32[]{:S(2)}) async-start(), calls=%async_computation.5 | async-start | bytes 3620864 | tf_op jit(solution)/shard_map/all_gather | solution.py:51
  9.0 18.5 %copy-start.10 = (bf16[2,1,128,1600]{2,3,1,0:T(8,128)(2,1)S(1)}, bf16[2,1,128,1600]{2,3,1,0:T(8,128)(2,1)}, u32[]{:S(2)}) copy-start(bf16[2,1,128,1600]{2,3,1,0:T(8,128)(2,1)} %param.18) | copy-start | bytes 2457604
  27.0 57.4 %copy-start = (bf16[1,2,1,128,1600]{4,3,2,1,0:T(8,128)(2,1)}, bf16[1,2,1,128,1600]{4,3,2,1,0:T(8,128)(2,1)S(1)}, u32[]{:S(2)}) copy-start(bf16[1,2,1,128,1600]{4,3,2,1,0:T(8,128)(2,1)S(1)} %all-gather) | copy-start | bytes 2457604
  27.3 57.2 %copy-start.39 = (f32[2,128]{1,0:T(2,128)}, f32[2,128]{1,0:T(2,128)S(1)}, u32[]{:S(2)}) copy-start(f32[2,128]{1,0:T(2,128)S(1)} %add_rsqrt_fusion) | copy-start | bytes 3076
  28.4 50.4 %copy-start.21 = (bf16[3,1,128,1600]{2,3,0,1:T(8,128)(2,1)}, bf16[3,1,128,1600]{2,3,0,1:T(8,128)(2,1)S(1)}, u32[]{:S(2)}) copy-start(bf16[3,1,128,1600]{2,3,0,1:T(8,128)(2,1)S(1)} %get-tuple-element.409) | copy-start | bytes 3686404
  87.5 0.8 copy-start.27
  87.5 4.2 copy-start.26
  91.7 3.9 copy-start.33
  91.8 2.1 copy-start.12
  99.8 18.2 %all-to-all-start = ((bf16[1,8,16,1600]{3,2,0,1:T(8,128)(2,1)}), bf16[1,8,16,1600]{3,2,0,1:T(8,128)(2,1)}, u32[]{:S(2)}, u32[]{:S(2)}) async-start(bf16[1,8,16,1600]{3,2,0,1:T(8,128)(2,1)} %bitcast.591), calls=%async_computation | async-start | bytes 851968 | tf_op jit(solution)/shard_map/all_to_all | solution.py:138
  126.1 1.8 copy-start.2
  126.1 1.9 copy-start.6
  130.1 42.2 %collective-permute-start = (bf16[1,16,1600]{1,2,0:T(8,128)(2,1)}, bf16[1,16,1600]{1,2,0:T(8,128)(2,1)}, u32[]{:S(2)}, u32[]{:S(2)}) collective-permute-start(bf16[1,16,1600]{1,2,0:T(8,128)(2,1)} %fusion.121), channel_id=1, source_target_pairs={{128,0},{256,128},{384,256},{129,1},{257,129},{385,257},{130,2},{2... | collective-permute-start | bytes 153608 | tf_op jit(solution)/shard_map/ppermute | solution.py:20
  215.4 0.7 copy-start.22
  222.4 1.8 copy-start.3
  222.4 1.9 copy-start.7
  226.4 96.2 %collective-permute-start.1 = (bf16[1,16,1600]{1,2,0:T(8,128)(2,1)}, bf16[1,16,1600]{1,2,0:T(8,128)(2,1)}, u32[]{:S(2)}, u32[]{:S(2)}) collective-permute-start(bf16[1,16,1600]{1,2,0:T(8,128)(2,1)} %fusion.141), channel_id=1, source_target_pairs={{128,0},{256,128},{384,256},{129,1},{257,129},{385,257},{130,2},{2... | collective-permute-start | bytes 153608 | tf_op jit(solution)/shard_map/ppermute | solution.py:20
  372.3 0.7 copy-start.16
  378.3 17.4 %all-to-all-start.2 = ((bf16[1,8,16,1600]{3,2,0,1:T(8,128)(2,1)}), bf16[1,8,16,1600]{3,2,0,1:T(8,128)(2,1)}, u32[]{:S(2)}, u32[]{:S(2)}) async-start(bf16[1,8,16,1600]{3,2,0,1:T(8,128)(2,1)} %bitcast.592), calls=%async_computation.2 | async-start | bytes 851968 | tf_op jit(solution)/shard_map/all_to_all | solution.py:138
  396.8 0.6 copy-start.23
  403.9 1.8 copy-start.4
  403.9 1.9 copy-start.8
  405.7 4.8 copy-start.32
  407.2 0.8 copy-start.18
  407.9 42.0 %collective-permute-start.2 = (bf16[1,16,1600]{1,2,0:T(8,128)(2,1)S(1)}, bf16[1,16,1600]{1,2,0:T(8,128)(2,1)}, u32[]{:S(2)}, u32[]{:S(2)}) collective-permute-start(bf16[1,16,1600]{1,2,0:T(8,128)(2,1)S(1)} %fusion.136), channel_id=1, source_target_pairs={{128,0},{256,128},{384,256},{129,1},{257,129},{385,257},{130,2},{2... | collective-permute-start | bytes 153608 | tf_op jit(solution)/shard_map/ppermute | solution.py:20
  499.9 0.7 copy-start.17
  505.9 20.8 %all-to-all-start.3 = ((bf16[1,8,16,1600]{3,2,0,1:T(8,128)(2,1)}), bf16[1,8,16,1600]{3,2,0,1:T(8,128)(2,1)}, u32[]{:S(2)}, u32[]{:S(2)}) async-start(bf16[1,8,16,1600]{3,2,0,1:T(8,128)(2,1)} %bitcast.593), calls=%async_computation.3 | async-start | bytes 851968 | tf_op jit(solution)/shard_map/all_to_all | solution.py:138
  527.8 0.6 copy-start.24
  534.8 1.8 copy-start.5
  534.8 1.9 copy-start.9
  538.9 19.9 %collective-permute-start.3 = (bf16[1,16,1600]{1,2,0:T(8,128)(2,1)}, bf16[1,16,1600]{1,2,0:T(8,128)(2,1)}, u32[]{:S(2)}, u32[]{:S(2)}) collective-permute-start(bf16[1,16,1600]{1,2,0:T(8,128)(2,1)} %fusion.131), channel_id=1, source_target_pairs={{128,0},{256,128},{384,256},{129,1},{257,129},{385,257},{130,2},{2... | collective-permute-start | bytes 153608 | tf_op jit(solution)/shard_map/ppermute | solution.py:20
  604.4 8.8 %copy-start.1 = (bf16[1,2,1,128,1600]{4,3,2,1,0:T(8,128)(2,1)S(1)}, bf16[1,2,1,128,1600]{4,3,2,1,0:T(8,128)(2,1)}, u32[]{:S(2)}) copy-start(bf16[1,2,1,128,1600]{4,3,2,1,0:T(8,128)(2,1)} %copy-done) | copy-start | bytes 2457604
  604.4 8.8 %copy-start.40 = (f32[2,128]{1,0:T(2,128)S(1)}, f32[2,128]{1,0:T(2,128)}, u32[]{:S(2)}) copy-start(f32[2,128]{1,0:T(2,128)} %copy-done.39) | copy-start | bytes 3076
  606.5 113.7 %all-to-all-start.4 = ((bf16[1,8,16,1600]{3,2,0,1:T(8,128)(2,1)}), bf16[1,8,16,1600]{3,2,0,1:T(8,128)(2,1)}, u32[]{:S(2)}, u32[]{:S(2)}) async-start(bf16[1,8,16,1600]{3,2,0,1:T(8,128)(2,1)} %bitcast.152), calls=%async_computation.4 | async-start | bytes 851968 | tf_op jit(solution)/shard_map/all_to_all | solution.py:138
  613.2 3.7 copy-start.11
  704.0 11.5 %copy-start.20 = (bf16[112,1024]{1,0:T(8,128)(2,1)S(1)}, bf16[112,1024]{1,0:T(8,128)(2,1)}, u32[]{:S(2)}) copy-start(bf16[112,1024]{1,0:T(8,128)(2,1)} %fusion) | copy-start | bytes 688132
  705.0 10.5 %collective-permute-start.4 = (bf16[112,1024]{1,0:T(8,128)(2,1)}, bf16[112,1024]{1,0:T(8,128)(2,1)S(1)}, u32[]{:S(2)}, u32[]{:S(2)}) collective-permute-start(bf16[112,1024]{1,0:T(8,128)(2,1)} %fusion), channel_id=1, source_target_pairs={{0,8},{8,16},{16,24},{24,32},{32,40},{40,48},{48,56},{56,64},{64,7... | collective-permute-start | bytes 688136
  708.6 6.8 collective-permute-start.5
  712.7 3.4 copy-start.19
  712.7 3.4 copy-start.28
  712.7 3.4 copy-start.29
  717.8 4.7 copy-start.35
  717.8 4.7 copy-start.36
  717.8 4.7 copy-start.37
  717.8 4.7 copy-start.38
  722.2 52.6 %copy-start.13 = (bf16[1,128,1600]{1,2,0:T(8,128)(2,1)S(1)}, bf16[1,128,1600]{1,2,0:T(8,128)(2,1)}, u32[]{:S(2)}) copy-start(bf16[1,128,1600]{1,2,0:T(8,128)(2,1)} %get-tuple-element.402) | copy-start | bytes 1228804
  722.2 52.6 %copy-start.41 = (f32[16]{0:T(128)S(1)}, f32[16]{0:T(128)}, u32[]{:S(2)}) copy-start(f32[16]{0:T(128)} %get-tuple-element.429) | copy-start | bytes 196
Sparse Core Ops, SparseCore 0:
  11.6 67.1 all-gather.3
